TPU v7x, 128 devices: a whole 4x4x4 slice. The times are simulated.
128 devices in a mesh: row: 8 (over z, y_hi), col: 16 (over x, y_lo, core).
Axes of the slice: x: 4, y: 4 (y_hi: 2, y_lo: 2; y = y_hi * 2 + y_lo), z: 4, core: 2. Of those that a mesh axis runs over, the one named last changes fastest.
Arguments:
- obj: float32 [2, 2048, 4096], P(None, 'row', 'col'), may hold values from -4.2 to 4.2
- probe: float32 [2, 256, 256], replicated, may hold values from -4.2 to 4.2
- amplitudes: bfloat16 [512, 256, 256], P(('row', 'col')), may hold values from 0.049804688 to 4
- positions: int32 [512, 2], replicated, may hold values from 0 to 3840, as said below
Outputs:
- new_object: float32 [2, 2048, 4096], P(None, 'row', 'col')
- new_probe: float32 [2, 256, 256], replicated
Inputs may be any that keep to these rules, and one draw needn't show every extreme that they name: `positions`: entry p is the top-left cell (row, column) of pattern p's window of 256 x 256 cells, which lies inside the object. Pattern p is held by device p // 4 in row-major order of (row, col), and its row offset lies in that device's band of 256 object rows. One device holds at most 2 patterns whose window starts in one tile, and exactly 2 for some tile in every draw; at most 8 windows start in one tile, and in every row of tiles exactly 8 start in one tile.
All inputs are finite; a program needn't handle non-finite values.
Results may differ from a plain program's by a relative error of at most 0.0018.
Values may be sent and summed in bfloat16 or wider, within the bound.
A program may use at most 128 MiB of HBM per device.

v0:
```python
import jax
import jax.numpy as jnp
from jax import lax
from jax.sharding import PartitionSpec as P

ITERS = 2
SEND = 2
amplitude_floor = 0.1
object_regular = 0.5
probe_regular = 1.0
highest = lax.Precision.HIGHEST


def passed_along(value, axis, steps):
    count = lax.axis_size(axis)
    leading, last = (max(0, -steps), min(count, count - steps))
    return lax.ppermute(value, axis, [(source, source + steps) for source in range(leading, last)])


def dft_tables(order):
    counter = jnp.arange(order, dtype=jnp.int32)
    phases = counter[:, None] * counter[None, :] % order
    angles = phases.astype(jnp.float32) * (2.0 * jnp.pi / order)
    norming = 1.0 / jnp.sqrt(jnp.float32(order))
    return (jnp.cos(angles) * norming, -jnp.sin(angles) * norming)


def left_apply(tables, real_part, imag_part):
    first = jnp.einsum("ab,sbc->sac", tables[0], real_part, precision=highest)
    second = jnp.einsum("ab,sbc->sac", tables[1], imag_part, precision=highest)
    third = jnp.einsum("ab,sbc->sac", tables[2], real_part + imag_part, precision=highest)
    return (first - second, third - first - second)


def right_apply(tables, real_part, imag_part):
    first = jnp.einsum("sab,bc->sac", real_part, tables[0], precision=highest)
    second = jnp.einsum("sab,bc->sac", imag_part, tables[1], precision=highest)
    third = jnp.einsum("sab,bc->sac", real_part + imag_part, tables[2], precision=highest)
    return (first - second, third - first - second)


def transform(tables, real_part, imag_part):
    inner_re, inner_im = right_apply(tables, real_part, imag_part)
    return left_apply(tables, inner_re, inner_im)


def extend_tile(current):
    from_right = passed_along(current, "col", -1)
    widened = jnp.concatenate([current, from_right], axis=2)
    from_below = passed_along(widened, "row", -1)
    return jnp.concatenate([widened, from_below], axis=1)


def fold_tile(sums, tile_rows, tile_cols, order):
    from_above = passed_along(sums[:, tile_rows:, :], "row", 1)
    upper = sums[:, :tile_rows, :].at[:, :order, :].add(from_above)
    from_left = passed_along(upper[:, :, tile_cols:], "col", 1)
    return upper[:, :, :tile_cols].at[:, :, :order].add(from_left)


def local(obj, probe, amplitudes, positions):
    col_count = lax.axis_size("col")
    my_row = lax.axis_index("row")
    my_col = lax.axis_index("col")
    device_id = my_row * col_count + my_col
    tile_rows = obj.shape[1]
    tile_cols = obj.shape[2]
    order = probe.shape[1]
    pat_count = amplitudes.shape[0]
    capacity = 2 * pat_count
    slot_count = col_count * SEND
    band_count = col_count * pat_count
    local_index = jnp.arange(pat_count, dtype=jnp.int32)
    my_ids = device_id * pat_count + local_index
    owner_col = positions[my_ids, 1] // tile_cols
    earlier = local_index[None, :] < local_index[:, None]
    same_owner = owner_col[:, None] == owner_col[None, :]
    send_rank = jnp.sum(same_owner & earlier, axis=1)
    send_slot = owner_col * SEND + send_rank
    placing = (jnp.arange(slot_count, dtype=jnp.int32)[:, None] == send_slot[None, :]).astype(
        jnp.bfloat16
    )
    outgoing = jnp.dot(
        placing, amplitudes.reshape(pat_count, order * order), preferred_element_type=jnp.float32
    ).astype(jnp.bfloat16)
    incoming = lax.all_to_all(outgoing, "col", split_axis=0, concat_axis=0, tiled=True)
    band_first = my_row * band_count
    band_pos = lax.dynamic_slice_in_dim(positions, band_first, band_count, 0)
    band_ids = band_first + jnp.arange(band_count, dtype=jnp.int32)
    in_mine = band_pos[:, 1] // tile_cols == my_col
    mine_count = in_mine.astype(jnp.int32)
    band_rank = jnp.cumsum(mine_count) - mine_count
    selection = (band_rank[None, :] == jnp.arange(capacity, dtype=jnp.int32)[:, None]) & in_mine[
        None, :
    ]
    valid = jnp.any(selection, axis=1)
    listed = jnp.sum(jnp.where(selection, band_ids[None, :], 0), axis=1)
    source_dev = listed // pat_count
    source_col = source_dev % col_count
    before = (
        (source_dev[None, :] == source_dev[:, None])
        & (listed[None, :] < listed[:, None])
        & valid[None, :]
    )
    recv_rank = jnp.sum(before, axis=1)
    recv_slot = source_col * SEND + recv_rank
    picking = (
        (jnp.arange(slot_count, dtype=jnp.int32)[None, :] == recv_slot[:, None]) & valid[:, None]
    ).astype(jnp.bfloat16)
    measured = jnp.dot(picking, incoming, preferred_element_type=jnp.float32).reshape(
        capacity, order, order
    )
    spots = positions[listed]
    offset_y = jnp.where(valid, spots[:, 0] - my_row * tile_rows, 0)
    offset_x = jnp.where(valid, spots[:, 1] - my_col * tile_cols, 0)
    weight = valid.astype(jnp.float32)[:, None, None]
    cos_part, sin_part = dft_tables(order)
    forward = (cos_part, sin_part, cos_part + sin_part)
    inverse = (cos_part, -sin_part, cos_part - sin_part)
    current = obj
    probe_now = probe
    for sweep in range(ITERS):
        extended = extend_tile(current)

        def cut_window(top, left):
            return lax.dynamic_slice(extended, (0, top, left), (2, order, order))

        windows = jax.vmap(cut_window)(offset_y, offset_x)
        win_re = windows[:, 0]
        win_im = windows[:, 1]
        probe_re = probe_now[0]
        probe_im = probe_now[1]
        exit_re = probe_re * win_re - probe_im * win_im
        exit_im = probe_re * win_im + probe_im * win_re
        far_re, far_im = transform(forward, exit_re, exit_im)
        factor = measured / jnp.sqrt(far_re * far_re + far_im * far_im + amplitude_floor)
        back_re, back_im = transform(inverse, far_re * factor, far_im * factor)
        change_re = (back_re - exit_re) * weight
        change_im = (back_im - exit_im) * weight
        power = probe_re * probe_re + probe_im * probe_im
        deposits = jnp.stack(
            [
                probe_re * change_re + probe_im * change_im,
                probe_re * change_im - probe_im * change_re,
                power[None] * weight + 0.0 * change_re,
            ],
            axis=1,
        )

        def deposit(index, total):
            start = (0, offset_y[index], offset_x[index])
            block = lax.dynamic_slice(total, start, (3, order, order))
            return lax.dynamic_update_slice(total, block + deposits[index], start)

        sums = lax.fori_loop(
            0, capacity, deposit, jnp.zeros((3, tile_rows + order, tile_cols + order), jnp.float32)
        )
        partials = jnp.stack(
            [
                jnp.sum(win_re * change_re + win_im * change_im, axis=0),
                jnp.sum(win_re * change_im - win_im * change_re, axis=0),
                jnp.sum((win_re * win_re + win_im * win_im) * weight, axis=0),
            ]
        )
        tile_sums = fold_tile(sums, tile_rows, tile_cols, order)
        current = current + tile_sums[:2] / (tile_sums[2] + object_regular)[None]
        totals = lax.psum(partials, ("row", "col"))
        probe_now = probe_now + totals[:2] / (totals[2] + probe_regular)[None]
    return (current, probe_now)


def solution(mesh):
    placed = (P(None, "row", "col"), P(), P(("row", "col"), None, None), P())
    return jax.shard_map(
        local, mesh=mesh, in_specs=placed, out_specs=(P(None, "row", "col"), P()), check_vma=False
    )
```

profile of v0, /device:TPU:1, one launch (start us, length us, event | category | flops | bytes accessed | tf_op | source)
XLA Modules:
  0.0 974.0 jit_solution(13523694036995378047)
XLA Ops:
  34.0 65.7 %collective-permute-done.1 = f32[2,256,512]{2,1,0:T(8,128)} collective-permute-done((f32[2,256,512]{2,1,0:T(8,128)S(1)}, f32[2,256,512]{2,1,0:T(8,128)}, u32[]{:S(2)}, u32[]{:S(2)}) %collective-permute-start.1) | collective-permute-done | bytes 1048608 | tf_op jit(solution)/shard_map/ppermute | solution.py:17
  103.5 25.5 %while.38 = (s32[]{:T(128)}, f32[2,512,512]{2,1,0:T(8,128)S(1)}, s32[8,3]{0,1:T(4,128)S(1)}, f32[8,2,256,256]{2,3,0,1:T(8,128)}, s32[]{:T(128)}) while((s32[]{:T(128)}, f32[2,512,512]{2,1,0:T(8,128)S(1)}, s32[8,3]{0,1:T(4,128)S(1)}, f32[8,2,256,256]{2,3,0,1:T(8,128)}, s32[]{:T(128)}) %tuple.156), condition=%wide.while_cond.4, body=%wide.while_body.4.sunk | while | flops 2 | bytes 3145853 | solution.py:126
  169.6 12.4 %fusion.48 = (f32[8,256,256]{1,2,0:T(8,128)S(1)}, f32[8,256,256]{1,2,0:T(8,128)S(1)}) fusion(f32[8,256,256]{1,2,0:T(8,128)} %copy.167, f32[8,256,256]{2,1,0:T(8,128)} %fusion.112, f32[8,256,256]{2,1,0:T(8,128)} %fusion.79, f32[8,256,256]{2,1,0:T(8,128)} %copy-done.9, f32[8,256,256]{2,1,0:T(8,128)} %copy-done.4, f32[8,256,256]{2,1,0:T(8,128)} %copy-done.3), kind=kOutput, calls=%fused_computation.104 | convolution fusion | flops 1618083840 | bytes 16777216 | tf_op jit(solution)/shard_map/ab,sbc->sac/dot_general | solution.py:31
  204.8 6.5 fusion.27
  217.5 134.4 %while.36 = (s32[]{:T(128)}, f32[3,512,512]{2,1,0:T(8,128)}, s32[8]{0:T(128)S(1)}, s32[8]{0:T(128)S(1)}, f32[8,3,256,256]{2,3,0,1:T(8,128)}, /*index=5*/s32[]{:T(128)}, s32[]{:T(128)}, s32[]{:T(128)}) while((s32[]{:T(128)}, f32[3,512,512]{2,1,0:T(8,128)}, s32[8]{0:T(128)S(1)}, s32[8]{0:T(128)S(1)}, f32[8,3,256,256]{2,3,0,1:T(8,128)}, ...), condition=%wide.region_6.7_spmd, body=%wide.region_5.6_spmd.sunk | while | flops 196616 | bytes 7078089 | solution.py:155
  225.6 8.9 dynamic_update_slice.16
  242.7 8.9 dynamic_update_slice.16
  259.7 9.4 dynamic_update_slice.16
  277.2 9.0 dynamic_update_slice.16
  294.3 8.3 dynamic_update_slice.16
  310.7 8.3 dynamic_update_slice.16
  327.2 8.3 dynamic_update_slice.16
  343.6 8.3 dynamic_update_slice.16
  357.5 31.8 %collective-permute-done.2 = f32[3,256,512]{2,1,0:T(8,128)S(1)} collective-permute-done((f32[3,256,512]{2,1,0:T(8,128)S(1)}, f32[3,256,512]{2,1,0:T(8,128)S(1)}, u32[]{:S(2)}, u32[]{:S(2)}) %collective-permute-start.2) | collective-permute-done | bytes 1572896 | tf_op jit(solution)/shard_map/ppermute | solution.py:17
  389.7 6.2 collective-permute-start.3
  396.0 8.9 collective-permute-done.3
  408.2 8.3 collective-permute-done.4
  418.1 147.8 %all-reduce.4.cloned.1.call-done = f32[3,256,256]{1,2,0:T(8,128)} async-done(((f32[3,256,256]{1,2,0:T(8,128)}), f32[3,256,256]{1,2,0:T(8,128)}) %all-reduce.4.cloned.1.call-update) | async-done | bytes 786448 | tf_op jit(solution)/shard_map/psum | solution.py:167
  572.9 25.8 %while.39 = (s32[]{:T(128)}, f32[2,512,512]{2,1,0:T(8,128)S(1)}, s32[8,3]{0,1:T(4,128)S(1)}, f32[8,2,256,256]{2,3,0,1:T(8,128)}, s32[]{:T(128)}) while((s32[]{:T(128)}, f32[2,512,512]{2,1,0:T(8,128)S(1)}, s32[8,3]{0,1:T(4,128)S(1)}, f32[8,2,256,256]{2,3,0,1:T(8,128)}, s32[]{:T(128)}) %tuple.172), condition=%wide.while_cond.5, body=%wide.while_body.5.sunk | while | flops 2 | bytes 3145853 | solution.py:126
  652.9 6.9 fusion.12
  666.0 133.6 %while.37 = (s32[]{:T(128)}, f32[3,512,512]{2,1,0:T(8,128)}, s32[8]{0:T(128)S(1)}, s32[8]{0:T(128)S(1)}, f32[8,3,256,256]{2,3,0,1:T(8,128)}, /*index=5*/s32[]{:T(128)}, s32[]{:T(128)}, s32[]{:T(128)}) while((s32[]{:T(128)}, f32[3,512,512]{2,1,0:T(8,128)}, s32[8]{0:T(128)S(1)}, s32[8]{0:T(128)S(1)}, f32[8,3,256,256]{2,3,0,1:T(8,128)}, ...), condition=%wide.region_12.13_spmd, body=%wide.region_11.12_spmd.sunk | while | flops 196616 | bytes 7078089 | solution.py:155
  674.0 8.9 dynamic_update_slice.17
  690.9 8.9 dynamic_update_slice.17
  707.9 9.4 dynamic_update_slice.17
  725.3 9.0 dynamic_update_slice.17
  742.3 8.3 dynamic_update_slice.17
  758.6 8.3 dynamic_update_slice.17
  775.0 8.3 dynamic_update_slice.17
  791.3 8.3 dynamic_update_slice.17
  808.5 30.1 %collective-permute-done.6 = f32[3,256,512]{2,1,0:T(8,128)} collective-permute-done((f32[3,256,512]{2,1,0:T(8,128)}, f32[3,256,512]{2,1,0:T(8,128)}, u32[]{:S(2)}, u32[]{:S(2)}) %collective-permute-start.6) | collective-permute-done | bytes 1572896 | tf_op jit(solution)/shard_map/ppermute | solution.py:17
  841.6 5.9 collective-permute-start.7
  847.6 114.0 %all-reduce.6.cloned.1.call-done = f32[3,256,256]{1,2,0:T(8,128)} async-done(((f32[3,256,256]{1,2,0:T(8,128)}), f32[3,256,256]{1,2,0:T(8,128)}) %all-reduce.6.cloned.1.call-update) | async-done | bytes 786448 | tf_op jit(solution)/shard_map/psum | solution.py:167
  (330 shorter events, 313.4 us)
Async XLA Ops:
  7.2 23.1 %collective-permute-start = (f32[2,256,256]{2,1,0:T(8,128)}, f32[2,256,256]{2,1,0:T(8,128)S(1)}, u32[]{:S(2)}, u32[]{:S(2)}) collective-permute-start(f32[2,256,256]{2,1,0:T(8,128)} %param.24), channel_id=1, source_target_pairs={{1,0},{2,1},{3,2},{4,3},{5,4},{6,5},{7,6},{8,7},{9,8},{10,9},{11,1... | collective-permute-start | bytes 1572872 | tf_op jit(solution)/shard_map/ppermute | solution.py:17
  22.6 5.7 copy-start
  22.6 7.4 copy-start.19
  22.6 134.4 %all-to-all-start = ((bf16[16,2,65536]{2,1,0:T(2,128)(2,1)}), bf16[16,2,65536]{2,1,0:T(2,128)(2,1)}, u32[]{:S(2)}, u32[]{:S(2)}) async-start(bf16[16,2,65536]{2,1,0:T(2,128)(2,1)} %all_to_all.8), calls=%async_computation | async-start | bytes 8388608 | tf_op jit(solution)/shard_map/all_to_all | solution.py:86
  28.3 537.6 %all-reduce.4.cloned.1.call-start = ((), (), s32[]{:S(2)}) async-start(), calls=%async_computation.1 | async-start | bytes 1572864 | tf_op jit(solution)/shard_map/psum | solution.py:167
  30.4 69.3 %collective-permute-start.1 = (f32[2,256,512]{2,1,0:T(8,128)S(1)}, f32[2,256,512]{2,1,0:T(8,128)}, u32[]{:S(2)}, u32[]{:S(2)}) collective-permute-start(f32[2,256,512]{2,1,0:T(8,128)S(1)} %constant_dynamic-update-slice_fusion.2), channel_id=1, source_target_pairs={{16,0},{32,16},{48,32},{64,48},{80,64},{96,80},{112,96},{17,1},{33... | collective-permute-start | bytes 3145736 | tf_op jit(solution)/shard_map/ppermute | solution.py:17
  131.8 8.9 copy-start.1
  136.2 15.1 %copy-start.3 = (f32[8,256,256]{2,1,0:T(8,128)}, f32[8,256,256]{2,1,0:T(8,128)S(1)}, u32[]{:S(2)}) copy-start(f32[8,256,256]{2,1,0:T(8,128)S(1)} %fusion.114) | copy-start | bytes 6291460
  140.7 10.6 %copy-start.4 = (f32[8,256,256]{2,1,0:T(8,128)}, f32[8,256,256]{2,1,0:T(8,128)S(1)}, u32[]{:S(2)}) copy-start(f32[8,256,256]{2,1,0:T(8,128)S(1)} %fusion.126) | copy-start | bytes 6291460
  145.7 5.6 copy-start.9
  195.8 9.0 copy-start.7
  204.8 6.5 copy-start.18
  204.8 6.5 copy-start.29
  352.0 37.3 %copy-start.6 = (f32[3,512,512]{2,1,0:T(8,128)S(1)}, f32[3,512,512]{2,1,0:T(8,128)}, u32[]{:S(2)}) copy-start(f32[3,512,512]{2,1,0:T(8,128)} %get-tuple-element.270) | copy-start | bytes 9437188
  353.7 35.6 %collective-permute-start.2 = (f32[3,256,512]{2,1,0:T(8,128)S(1)}, f32[3,256,512]{2,1,0:T(8,128)S(1)}, u32[]{:S(2)}, u32[]{:S(2)}) collective-permute-start(f32[3,256,512]{2,1,0:T(8,128)S(1)} %slice.165), channel_id=1, source_target_pairs={{0,16},{16,32},{32,48},{48,64},{64,80},{80,96},{96,112},{1,17},{17... | collective-permute-start | bytes 4718600 | tf_op jit(solution)/shard_map/ppermute | solution.py:17
  389.6 15.4 %copy-start.20 = (f32[2,256,256]{2,1,0:T(8,128)S(1)}, f32[2,256,256]{2,1,0:T(8,128)}, u32[]{:S(2)}) copy-start(f32[2,256,256]{2,1,0:T(8,128)} %param.24) | copy-start | bytes 1572868
  389.7 15.2 %collective-permute-start.3 = (f32[3,256,256]{2,1,0:T(8,128)S(1)}, f32[3,256,256]{2,1,0:T(8,128)S(1)}, u32[]{:S(2)}, u32[]{:S(2)}) collective-permute-start(f32[3,256,256]{2,1,0:T(8,128)S(1)} %slice.219), channel_id=1, source_target_pairs={{0,1},{1,2},{2,3},{3,4},{4,5},{5,6},{6,7},{7,8},{8,9},{9,10},{10,1... | collective-permute-start | bytes 2359304 | tf_op jit(solution)/shard_map/ppermute | solution.py:17
  405.2 163.9 %copy-start.11 = (f32[2,256,256]{2,1,0:T(8,128)}, f32[2,256,256]{2,1,0:T(8,128)S(1)}, u32[]{:S(2)}) copy-start(f32[2,256,256]{2,1,0:T(8,128)S(1)} %fusion.84) | copy-start | bytes 1572868
  405.2 11.2 %collective-permute-start.4 = (f32[2,256,256]{2,1,0:T(8,128)S(1)}, f32[2,256,256]{2,1,0:T(8,128)S(1)}, u32[]{:S(2)}, u32[]{:S(2)}) collective-permute-start(f32[2,256,256]{2,1,0:T(8,128)S(1)} %fusion.84), channel_id=1, source_target_pairs={{1,0},{2,1},{3,2},{4,3},{5,4},{6,5},{7,6},{8,7},{9,8},{10,9},{11,1... | collective-permute-start | bytes 1572872 | tf_op jit(solution)/shard_map/ppermute | solution.py:17
  407.1 10.8 %copy-start.22 = (f32[2,256,256]{2,1,0:T(8,128)S(1)}, f32[2,256,256]{2,1,0:T(8,128)}, u32[]{:S(2)}) copy-start(f32[2,256,256]{2,1,0:T(8,128)} %param.25) | copy-start | bytes 1572868
  408.1 553.5 %all-reduce.6.cloned.1.call-start = ((), (), s32[]{:S(2)}) async-start(), calls=%async_computation.2 | async-start | bytes 1572864 | tf_op jit(solution)/shard_map/psum | solution.py:167
  416.6 152.5 %collective-permute-start.5 = (f32[2,256,512]{2,1,0:T(8,128)S(1)}, f32[2,256,512]{2,1,0:T(8,128)}, u32[]{:S(2)}, u32[]{:S(2)}) collective-permute-start(f32[2,256,512]{2,1,0:T(8,128)S(1)} %pad_maximum_fusion.4), channel_id=1, source_target_pairs={{16,0},{32,16},{48,32},{64,48},{80,64},{96,80},{112,96},{17,1},{33... | collective-permute-start | bytes 3145736 | tf_op jit(solution)/shard_map/ppermute | solution.py:17
  652.8 6.9 copy-start.17
  652.8 6.9 copy-start.28
  799.7 7.9 copy-start.25
  799.7 7.9 copy-start.26
  799.7 7.9 copy-start.27
  799.7 38.9 %copy-start.5 = (f32[3,512,512]{2,1,0:T(8,128)S(1)}, f32[3,512,512]{2,1,0:T(8,128)}, u32[]{:S(2)}) copy-start(f32[3,512,512]{2,1,0:T(8,128)} %get-tuple-element.271) | copy-start | bytes 9437188
  802.5 36.1 %collective-permute-start.6 = (f32[3,256,512]{2,1,0:T(8,128)}, f32[3,256,512]{2,1,0:T(8,128)}, u32[]{:S(2)}, u32[]{:S(2)}) collective-permute-start(f32[3,256,512]{2,1,0:T(8,128)} %slice.177), channel_id=1, source_target_pairs={{0,16},{16,32},{32,48},{48,64},{64,80},{80,96},{96,112},{1,17},{17... | collective-permute-start | bytes 4718600 | tf_op jit(solution)/shard_map/ppermute | solution.py:17
  841.5 121.0 %copy-start.16 = (f32[2,256,256]{1,2,0:T(8,128)S(1)}, f32[2,256,256]{1,2,0:T(8,128)}, u32[]{:S(2)}) copy-start(f32[2,256,256]{1,2,0:T(8,128)} %copy-done.15) | copy-start | bytes 1572868
  841.6 123.1 %copy-start.14 = (f32[3,256,512]{2,1,0:T(8,128)S(1)}, f32[3,256,512]{2,1,0:T(8,128)}, u32[]{:S(2)}) copy-start(f32[3,256,512]{2,1,0:T(8,128)} %copy-done.13) | copy-start | bytes 4718596
  841.6 123.1 %collective-permute-start.7 = (f32[3,256,256]{2,1,0:T(8,128)S(1)}, f32[3,256,256]{2,1,0:T(8,128)}, u32[]{:S(2)}, u32[]{:S(2)}) collective-permute-start(f32[3,256,256]{2,1,0:T(8,128)S(1)} %slice.227), channel_id=1, source_target_pairs={{0,1},{1,2},{2,3},{3,4},{4,5},{5,6},{6,7},{7,8},{8,9},{9,10},{10,1... | collective-permute-start | bytes 2359304 | tf_op jit(solution)/shard_map/ppermute | solution.py:17
  (9 other events, 26.3 us)
Sparse Core Ops, SparseCore 0:
  408.2 157.6 all-reduce.3
  808.6 152.9 all-reduce.5
where the time goes:
time: 985 us; the launch traced here: 974 us
  waiting for transfers between devices  407 us (41%)
  local copies, waits for them, and re-layouts  268 us (27%)
  matrix products  132 us (13%)
  loops' own time  61.9 us (6%)
  other arithmetic  55.1 us (6%)
  starting transfers between devices  34.6 us (4%)
  between operations  15.1 us (2%)
    psum x2, waiting for transfers between devices, local(): totals = lax.psum(partials, ('row', 'col'))  262 us
    ppermute x8, waiting for transfers between devices, passed_along(): lax.ppermute(value, axis, [(source, source + steps) for source in range(l...  145 us
    dynamic_update_slice x16, local copies, waits for them, and re-layouts, deposit(): return lax.dynamic_update_slice(total, block + deposits[index], start)  139 us
    another operation x2, loops' own time, local(): lax.fori_loop(0, capacity, deposit, jnp.zeros((3, tile_rows + order, tile...  61.4 us
    gather x80, local copies, waits for them, and re-layouts  50.8 us
    dot_general x4, matrix products, left_apply(): jnp.einsum('ab,sbc->sac', tables[2], real_part + imag_part, precision=hig...  31.3 us
    ppermute x8, starting transfers between devices, passed_along(): lax.ppermute(value, axis, [(source, source + steps) for source in range(l...  28.9 us
    add x16, other arithmetic, deposit(): return lax.dynamic_update_slice(total, block + deposits[index], start)  25.4 us
  transfers between devices with their start and end apart: 11, of which 7 were waited for; matrix products, arithmetic and copies ran while one was open for 8% of the time, Pallas kernels for 0%

commit v1 on v0

--- a/solution.py
+++ b/solution.py
@@ -164,7 +164,7 @@
         )
         tile_sums = fold_tile(sums, tile_rows, tile_cols, order)
         current = current + tile_sums[:2] / (tile_sums[2] + object_regular)[None]
-        totals = lax.psum(partials, ("row", "col"))
+        totals = lax.psum(lax.psum(partials, "row"), "col")
         probe_now = probe_now + totals[:2] / (totals[2] + probe_regular)[None]
     return (current, probe_now)
 

time: 985 us -> 1090 us (1.11)
  waiting for transfers between devices: 407 us -> 505 us
    psum x2 -> x4, waiting for transfers between devices: 262 us -> 399 us  [local(): totals = lax.psum(lax.psum(partials, 'row'), 'col')]
    ppermute x8, waiting for transfers between devices: 145 us -> 106 us  [passed_along(): lax.ppermute(value, axis, [(source, source + steps) for source in range(l...]
  transfers between devices with their start and end apart: 11 -> 13, of which waited for: 7 -> 7; matrix products, arithmetic and copies ran while one was open for 8% -> 7% of each run, Pallas kernels for 0% -> 0%
where the time goes in v1:
time: 1090 us; the launch traced here: 1080 us
  waiting for transfers between devices  505 us (46%)
  local copies, waits for them, and re-layouts  269 us (25%)
  matrix products  132 us (12%)
  loops' own time  61.9 us (6%)
  other arithmetic  56.2 us (5%)
  starting transfers between devices  37.7 us (3%)
  between operations  14.8 us (1%)
    psum x4, waiting for transfers between devices, local(): totals = lax.psum(lax.psum(partials, 'row'), 'col')  399 us
    dynamic_update_slice x16, local copies, waits for them, and re-layouts, deposit(): return lax.dynamic_update_slice(total, block + deposits[index], start)  139 us
    ppermute x8, waiting for transfers between devices, passed_along(): lax.ppermute(value, axis, [(source, source + steps) for source in range(l...  106 us
    another operation x2, loops' own time, local(): lax.fori_loop(0, capacity, deposit, jnp.zeros((3, tile_rows + order, tile...  61.4 us
    gather x80, local copies, waits for them, and re-layouts  50.8 us
    ppermute x8, starting transfers between devices, passed_along(): lax.ppermute(value, axis, [(source, source + steps) for source in range(l...  31.9 us
    dot_general x4, matrix products, left_apply(): jnp.einsum('ab,sbc->sac', tables[2], real_part + imag_part, precision=hig...  31.3 us
    add x16, other arithmetic, deposit(): return lax.dynamic_update_slice(total, block + deposits[index], start)  25.4 us
  transfers between devices with their start and end apart: 13, of which 7 were waited for; matrix products, arithmetic and copies ran while one was open for 7% of the time, Pallas kernels for 0%

profile of v1, /device:TPU:1, one launch (start us, length us, event | category | flops | bytes accessed | tf_op | source)
XLA Modules:
  0.0 1076.8 jit_solution(1513861480384165769)
XLA Ops:
  34.0 65.7 %collective-permute-done.1 = f32[2,256,512]{2,1,0:T(8,128)} collective-permute-done((f32[2,256,512]{2,1,0:T(8,128)S(1)}, f32[2,256,512]{2,1,0:T(8,128)}, u32[]{:S(2)}, u32[]{:S(2)}) %collective-permute-start.1) | collective-permute-done | bytes 1048608 | tf_op jit(solution)/shard_map/ppermute | solution.py:17
  103.5 25.5 %while.38 = (s32[]{:T(128)}, f32[2,512,512]{2,1,0:T(8,128)S(1)}, s32[8,3]{0,1:T(4,128)S(1)}, f32[8,2,256,256]{2,3,0,1:T(8,128)}, s32[]{:T(128)}) while((s32[]{:T(128)}, f32[2,512,512]{2,1,0:T(8,128)S(1)}, s32[8,3]{0,1:T(4,128)S(1)}, f32[8,2,256,256]{2,3,0,1:T(8,128)}, s32[]{:T(128)}) %tuple.156), condition=%wide.while_cond.4, body=%wide.while_body.4.sunk | while | flops 2 | bytes 3145853 | solution.py:126
  169.6 12.4 %fusion.48 = (f32[8,256,256]{1,2,0:T(8,128)S(1)}, f32[8,256,256]{1,2,0:T(8,128)S(1)}) fusion(f32[8,256,256]{1,2,0:T(8,128)} %copy.167, f32[8,256,256]{2,1,0:T(8,128)} %fusion.112, f32[8,256,256]{2,1,0:T(8,128)} %fusion.79, f32[8,256,256]{2,1,0:T(8,128)} %copy-done.9, f32[8,256,256]{2,1,0:T(8,128)} %copy-done.4, f32[8,256,256]{2,1,0:T(8,128)} %copy-done.3), kind=kOutput, calls=%fused_computation.104 | convolution fusion | flops 1618083840 | bytes 16777216 | tf_op jit(solution)/shard_map/ab,sbc->sac/dot_general | solution.py:31
  204.8 6.5 fusion.27
  217.5 134.4 %while.36 = (s32[]{:T(128)}, f32[3,512,512]{2,1,0:T(8,128)}, s32[8]{0:T(128)S(1)}, s32[8]{0:T(128)S(1)}, f32[8,3,256,256]{2,3,0,1:T(8,128)}, /*index=5*/s32[]{:T(128)}, s32[]{:T(128)}, s32[]{:T(128)}) while((s32[]{:T(128)}, f32[3,512,512]{2,1,0:T(8,128)}, s32[8]{0:T(128)S(1)}, s32[8]{0:T(128)S(1)}, f32[8,3,256,256]{2,3,0,1:T(8,128)}, ...), condition=%wide.region_6.7_spmd, body=%wide.region_5.6_spmd.sunk | while | flops 196616 | bytes 7078089 | solution.py:155
  225.6 8.9 dynamic_update_slice.16
  242.7 8.9 dynamic_update_slice.16
  259.7 9.4 dynamic_update_slice.16
  277.2 9.0 dynamic_update_slice.16
  294.3 8.3 dynamic_update_slice.16
  310.7 8.3 dynamic_update_slice.16
  327.2 8.3 dynamic_update_slice.16
  343.6 8.3 dynamic_update_slice.16
  357.5 31.8 %collective-permute-done.2 = f32[3,256,512]{2,1,0:T(8,128)S(1)} collective-permute-done((f32[3,256,512]{2,1,0:T(8,128)S(1)}, f32[3,256,512]{2,1,0:T(8,128)S(1)}, u32[]{:S(2)}, u32[]{:S(2)}) %collective-permute-start.2) | collective-permute-done | bytes 1572896 | tf_op jit(solution)/shard_map/ppermute | solution.py:17
  390.6 6.1 collective-permute-start.3
  397.7 8.2 collective-permute-done.3
  409.5 77.4 %all-reduce.6.cloned.1.call-done = f32[3,256,256]{1,2,0:T(8,128)} async-done(((f32[3,256,256]{1,2,0:T(8,128)}), f32[3,256,256]{1,2,0:T(8,128)}) %all-reduce.6.cloned.1.call-update) | async-done | bytes 786448 | tf_op jit(solution)/shard_map/psum | solution.py:167
  488.6 123.1 %all-reduce.8.cloned.1.call-done = f32[3,256,256]{1,2,0:T(8,128)} async-done(((f32[3,256,256]{1,2,0:T(8,128)}), f32[3,256,256]{1,2,0:T(8,128)}) %all-reduce.8.cloned.1.call-update) | async-done | bytes 786448 | tf_op jit(solution)/shard_map/psum | solution.py:167
  618.6 25.8 %while.39 = (s32[]{:T(128)}, f32[2,512,512]{2,1,0:T(8,128)S(1)}, s32[8,3]{0,1:T(4,128)S(1)}, f32[8,2,256,256]{2,3,0,1:T(8,128)}, s32[]{:T(128)}) while((s32[]{:T(128)}, f32[2,512,512]{2,1,0:T(8,128)S(1)}, s32[8,3]{0,1:T(4,128)S(1)}, f32[8,2,256,256]{2,3,0,1:T(8,128)}, s32[]{:T(128)}) %tuple.176), condition=%wide.while_cond.5, body=%wide.while_body.5.sunk | while | flops 2 | bytes 3145853 | solution.py:126
  698.6 6.9 fusion.12
  711.8 133.6 %while.37 = (s32[]{:T(128)}, f32[3,512,512]{2,1,0:T(8,128)}, s32[8]{0:T(128)S(1)}, s32[8]{0:T(128)S(1)}, f32[8,3,256,256]{2,3,0,1:T(8,128)}, /*index=5*/s32[]{:T(128)}, s32[]{:T(128)}, s32[]{:T(128)}) while((s32[]{:T(128)}, f32[3,512,512]{2,1,0:T(8,128)}, s32[8]{0:T(128)S(1)}, s32[8]{0:T(128)S(1)}, f32[8,3,256,256]{2,3,0,1:T(8,128)}, ...), condition=%wide.region_13.14_spmd, body=%wide.region_12.13_spmd.sunk | while | flops 196616 | bytes 7078089 | solution.py:155
  719.8 8.9 dynamic_update_slice.17
  736.7 8.9 dynamic_update_slice.17
  753.6 9.4 dynamic_update_slice.17
  771.0 9.0 dynamic_update_slice.17
  788.0 8.3 dynamic_update_slice.17
  804.4 8.3 dynamic_update_slice.17
  820.7 8.3 dynamic_update_slice.17
  837.1 8.3 dynamic_update_slice.17
  855.2 85.7 %all-reduce.10.cloned.1.call-done = f32[3,256,256]{1,2,0:T(8,128)} async-done(((f32[3,256,256]{1,2,0:T(8,128)}), f32[3,256,256]{1,2,0:T(8,128)}) %all-reduce.10.cloned.1.call-update) | async-done | bytes 786448 | tf_op jit(solution)/shard_map/psum | solution.py:167
  943.9 8.0 collective-permute-start.7
  951.9 112.8 %all-reduce.12.cloned.1.call-done = f32[3,256,256]{1,2,0:T(8,128)} async-done(((f32[3,256,256]{1,2,0:T(8,128)}), f32[3,256,256]{1,2,0:T(8,128)}) %all-reduce.12.cloned.1.call-update) | async-done | bytes 786448 | tf_op jit(solution)/shard_map/psum | solution.py:167
  (336 shorter events, 316.6 us)
Async XLA Ops:
  7.2 23.1 %collective-permute-start = (f32[2,256,256]{2,1,0:T(8,128)}, f32[2,256,256]{2,1,0:T(8,128)S(1)}, u32[]{:S(2)}, u32[]{:S(2)}) collective-permute-start(f32[2,256,256]{2,1,0:T(8,128)} %param.24), channel_id=1, source_target_pairs={{1,0},{2,1},{3,2},{4,3},{5,4},{6,5},{7,6},{8,7},{9,8},{10,9},{11,1... | collective-permute-start | bytes 1572872 | tf_op jit(solution)/shard_map/ppermute | solution.py:17
  22.6 7.4 copy-start.19
  22.6 134.4 %all-to-all-start = ((bf16[16,2,65536]{2,1,0:T(2,128)(2,1)}), bf16[16,2,65536]{2,1,0:T(2,128)(2,1)}, u32[]{:S(2)}, u32[]{:S(2)}) async-start(bf16[16,2,65536]{2,1,0:T(2,128)(2,1)} %all_to_all.8), calls=%async_computation | async-start | bytes 8388608 | tf_op jit(solution)/shard_map/all_to_all | solution.py:86
  28.3 458.5 %all-reduce.6.cloned.1.call-start = ((), (), s32[]{:S(2)}) async-start(), calls=%async_computation.1 | async-start | bytes 1572864 | tf_op jit(solution)/shard_map/psum | solution.py:167
  30.4 69.3 %collective-permute-start.1 = (f32[2,256,512]{2,1,0:T(8,128)S(1)}, f32[2,256,512]{2,1,0:T(8,128)}, u32[]{:S(2)}, u32[]{:S(2)}) collective-permute-start(f32[2,256,512]{2,1,0:T(8,128)S(1)} %constant_dynamic-update-slice_fusion.2), channel_id=1, source_target_pairs={{16,0},{32,16},{48,32},{64,48},{80,64},{96,80},{112,96},{17,1},{33... | collective-permute-start | bytes 3145736 | tf_op jit(solution)/shard_map/ppermute | solution.py:17
  131.8 8.9 copy-start.1
  136.2 15.1 %copy-start.3 = (f32[8,256,256]{2,1,0:T(8,128)}, f32[8,256,256]{2,1,0:T(8,128)S(1)}, u32[]{:S(2)}) copy-start(f32[8,256,256]{2,1,0:T(8,128)S(1)} %fusion.114) | copy-start | bytes 6291460
  140.7 10.6 copy-start.4
  195.8 9.0 copy-start.7
  204.8 6.5 copy-start.18
  204.8 6.5 copy-start.29
  352.0 37.3 %copy-start.6 = (f32[3,512,512]{2,1,0:T(8,128)S(1)}, f32[3,512,512]{2,1,0:T(8,128)}, u32[]{:S(2)}) copy-start(f32[3,512,512]{2,1,0:T(8,128)} %get-tuple-element.270) | copy-start | bytes 9437188
  353.7 35.6 %collective-permute-start.2 = (f32[3,256,512]{2,1,0:T(8,128)S(1)}, f32[3,256,512]{2,1,0:T(8,128)S(1)}, u32[]{:S(2)}, u32[]{:S(2)}) collective-permute-start(f32[3,256,512]{2,1,0:T(8,128)S(1)} %slice.165), channel_id=1, source_target_pairs={{0,16},{16,32},{32,48},{48,64},{64,80},{80,96},{96,112},{1,17},{17... | collective-permute-start | bytes 4718600 | tf_op jit(solution)/shard_map/ppermute | solution.py:17
  390.6 15.3 %collective-permute-start.3 = (f32[3,256,256]{2,1,0:T(8,128)}, f32[3,256,256]{2,1,0:T(8,128)}, u32[]{:S(2)}, u32[]{:S(2)}) collective-permute-start(f32[3,256,256]{2,1,0:T(8,128)} %slice.219), channel_id=1, source_target_pairs={{0,1},{1,2},{2,3},{3,4},{4,5},{5,6},{6,7},{7,8},{8,9},{9,10},{10,1... | collective-permute-start | bytes 2359304 | tf_op jit(solution)/shard_map/ppermute | solution.py:17
  397.7 9.6 copy-start.20
  397.7 214.0 %all-reduce.8.cloned.1.call-start = ((), (), s32[]{:S(2)}) async-start(), calls=%async_computation.2 | async-start | bytes 1572864 | tf_op jit(solution)/shard_map/psum | solution.py:167
  407.3 81.1 %copy-start.22 = (f32[2,256,256]{2,1,0:T(8,128)S(1)}, f32[2,256,256]{2,1,0:T(8,128)}, u32[]{:S(2)}) copy-start(f32[2,256,256]{2,1,0:T(8,128)} %param.25) | copy-start | bytes 1572868
  407.4 207.4 %copy-start.11 = (f32[2,256,256]{2,1,0:T(8,128)}, f32[2,256,256]{2,1,0:T(8,128)S(1)}, u32[]{:S(2)}) copy-start(f32[2,256,256]{2,1,0:T(8,128)S(1)} %fusion.84) | copy-start | bytes 1572868
  407.4 79.5 %collective-permute-start.4 = (f32[2,256,256]{2,1,0:T(8,128)S(1)}, f32[2,256,256]{2,1,0:T(8,128)S(1)}, u32[]{:S(2)}, u32[]{:S(2)}) collective-permute-start(f32[2,256,256]{2,1,0:T(8,128)S(1)} %fusion.84), channel_id=1, source_target_pairs={{1,0},{2,1},{3,2},{4,3},{5,4},{6,5},{7,6},{8,7},{9,8},{10,9},{11,1... | collective-permute-start | bytes 1572872 | tf_op jit(solution)/shard_map/ppermute | solution.py:17
  486.8 454.0 %all-reduce.10.cloned.1.call-start = ((), (), s32[]{:S(2)}) async-start(), calls=%async_computation.3 | async-start | bytes 1572864 | tf_op jit(solution)/shard_map/psum | solution.py:167
  487.1 127.8 %collective-permute-start.5 = (f32[2,256,512]{2,1,0:T(8,128)S(1)}, f32[2,256,512]{2,1,0:T(8,128)}, u32[]{:S(2)}, u32[]{:S(2)}) collective-permute-start(f32[2,256,512]{2,1,0:T(8,128)S(1)} %pad_maximum_fusion.4), channel_id=1, source_target_pairs={{16,0},{32,16},{48,32},{64,48},{80,64},{96,80},{112,96},{17,1},{33... | collective-permute-start | bytes 3145736 | tf_op jit(solution)/shard_map/ppermute | solution.py:17
  698.6 6.9 copy-start.17
  698.6 6.9 copy-start.28
  845.4 8.7 copy-start.25
  845.4 8.7 copy-start.26
  845.4 8.7 copy-start.27
  848.2 92.7 %copy-start.5 = (f32[3,512,512]{2,1,0:T(8,128)S(1)}, f32[3,512,512]{2,1,0:T(8,128)}, u32[]{:S(2)}) copy-start(f32[3,512,512]{2,1,0:T(8,128)} %get-tuple-element.271) | copy-start | bytes 9437188
  848.2 92.7 %collective-permute-start.6 = (f32[3,256,512]{2,1,0:T(8,128)}, f32[3,256,512]{2,1,0:T(8,128)}, u32[]{:S(2)}, u32[]{:S(2)}) collective-permute-start(f32[3,256,512]{2,1,0:T(8,128)} %slice.177), channel_id=1, source_target_pairs={{0,16},{16,32},{32,48},{48,64},{64,80},{80,96},{96,112},{1,17},{17... | collective-permute-start | bytes 4718600 | tf_op jit(solution)/shard_map/ppermute | solution.py:17
  855.1 209.6 %all-reduce.12.cloned.1.call-start = ((), (), s32[]{:S(2)}) async-start(), calls=%async_computation.4 | async-start | bytes 1572864 | tf_op jit(solution)/shard_map/psum | solution.py:167
  943.8 121.9 %copy-start.16 = (f32[2,256,256]{1,2,0:T(8,128)S(1)}, f32[2,256,256]{1,2,0:T(8,128)}, u32[]{:S(2)}) copy-start(f32[2,256,256]{1,2,0:T(8,128)} %copy-done.15) | copy-start | bytes 1572868
  943.9 123.9 %copy-start.14 = (f32[3,256,512]{2,1,0:T(8,128)S(1)}, f32[3,256,512]{2,1,0:T(8,128)}, u32[]{:S(2)}) copy-start(f32[3,256,512]{2,1,0:T(8,128)} %copy-done.13) | copy-start | bytes 4718596
  943.9 123.9 %collective-permute-start.7 = (f32[3,256,256]{2,1,0:T(8,128)S(1)}, f32[3,256,256]{2,1,0:T(8,128)}, u32[]{:S(2)}, u32[]{:S(2)}) collective-permute-start(f32[3,256,256]{2,1,0:T(8,128)S(1)} %slice.227), channel_id=1, source_target_pairs={{0,1},{1,2},{2,3},{3,4},{4,5},{5,6},{6,7},{7,8},{8,9},{9,10},{10,1... | collective-permute-start | bytes 2359304 | tf_op jit(solution)/shard_map/ppermute | solution.py:17
  (11 other events, 37.7 us)
Sparse Core Ops, SparseCore 0:
  397.8 88.9 all-reduce.5
  489.4 122.1 all-reduce.7
  855.2 85.5 all-reduce.9
  943.3 121.3 all-reduce.11
